TPU v7x, 512 devices: a whole 4x8x8 slice. The times are simulated.
512 devices in a mesh: segment: 8 (over x, core), kv: 64 (over y, z).
Axes of the slice: x: 4, y: 8, z: 8, core: 2. Of those that a mesh axis runs over, the one named last changes fastest.
Arguments:
- queries: bfloat16 [8, 64, 8192], P('segment', 'kv'), may hold values from -24 to 24
- new_key: bfloat16 [8, 64, 1024], P('segment', 'kv'), may hold values from -6 to 6
- new_value: bfloat16 [8, 64, 1024], P('segment', 'kv'), may hold values from -6 to 6
- key_pool: bfloat16 [8, 2048, 16, 1024], P('segment', 'kv'), may hold values from -16 to 16
- value_pool: bfloat16 [8, 2048, 16, 1024], P('segment', 'kv'), may hold values from -6 to 6
- lengths: int32 [8, 64], P('segment'), may hold values from 1 to 512, as said below
- block_device: int32 [8, 64, 32], P('segment'), may hold values from 0 to 63, as said below
- block_slot: int32 [8, 64, 32], P('segment'), may hold values from 0 to 31, as said below
- residual: bfloat16 [8, 64, 8192], P('segment', None, 'kv'), may hold values from -6 to 6
- out_weight: bfloat16 [8, 8192, 8192], P('segment', None, 'kv'), may hold values from -0.0625 to 0.0625
Outputs:
- passed: bfloat16 [8, 64, 8192], P('segment', None, 'kv')
Inputs may be any that keep to these rules, and one draw needn't show every extreme that they name: `lengths`: request 0 of every section has exactly 512 cached tokens. `block_device`: within a section, the live blocks of all requests (b * 16 < length) name distinct (instance, slot) pairs; entries past a request's length are arbitrary. `block_slot`: see block_device.
All inputs are finite; a program needn't handle non-finite values.
Results may differ from a plain program's by a relative error of at most 0.0035.
Values may be sent and summed in bfloat16 or wider, within the bound.
A program may use at most 64 MiB of HBM per device.

v0:
```python
import functools

import jax
import jax.numpy as jnp
from jax import lax
from jax.experimental import pallas as pl
from jax.experimental.pallas import tpu as pltpu
from jax.sharding import PartitionSpec as P

KV_HEADS = 8
HEAD_DIM = 128
HEADS = 64
HALF = HEADS // 2
PAIR = 16
BLK = 16
MESH = pl.DeviceIdType.MESH
EMPTY = -1e30
FLOOR = -1e29
SCALE = HEAD_DIM ** (-0.5)
LOG2_E = 1.4426950408889634

ASK_FIRST, PART, MERGED, TELL_FIRST = range(4)
ASK_SECOND, TELL_SECOND = range(2)

LEGS = (
    (0, None, 3, -3),
    (0, None, -3, 3),
    (0, None, 1, -1),
    (0, None, -1, 1),
    (-3, None, -1, -2),
    (3, None, 1, 2),
    (-3, 0, 1, -4),
    (3, 1, -1, 4),
)


def offsets(n):
    near = []
    for step in range(1, n // 2 + 1):
        near.append(step)
        if step != n - step:
            near.append(n - step)
    return near


def heads_in_row(raw, rows):
    flat = raw[0].astype(jnp.float32)
    for h in range(rows.shape[0]):
        rows[h : h + 1, :] = flat[:, h * HEAD_DIM : (h + 1) * HEAD_DIM]


def kernel(
    n_seg,
    n,
    q_hbm,
    nk_hbm,
    nv_hbm,
    len_hbm,
    dev_hbm,
    slot_hbm,
    res_hbm,
    k_hbm,
    v_hbm,
    w_hbm,
    out_ref,
    q_raw,
    nk_raw,
    nv_raw,
    len_buf,
    dev_buf,
    slot_buf,
    res_buf,
    rows64,
    q_ref,
    k_buf,
    v_buf,
    w_buf,
    kt_buf,
    bias_buf,
    q_all,
    part,
    got,
    merged,
    last,
    attn,
    told,
    rows32,
    told_all,
    turn,
    line,
    landed,
    send_sem,
    recv_sem,
    leg_send,
    leg_recv,
    load_sem,
    pass_sem,
):
    f32, bf16 = jnp.float32, jnp.bfloat16
    seg = lax.axis_index("segment")
    me = lax.axis_index("kv")
    y, z = lax.div(me, n), lax.rem(me, n)
    first, second = (z, y), (y, z)
    slots = k_buf.shape[0]
    tokens = slots * BLK
    rows = n * PAIR

    def at_first(half, i):
        return y * n + i if half == 0 else i * n + z

    def at_second(half, i):
        return i * n + z if half == 0 else y * n + i

    def peer(base, off):
        return lax.rem(base + off, n)

    def copy(stage, half, src, dst, device):
        return pltpu.make_async_remote_copy(
            src_ref=src,
            dst_ref=dst,
            send_sem=send_sem.at[stage, half],
            recv_sem=recv_sem.at[stage, half],
            device_id={"kv": device},
            device_id_type=MESH,
        )

    def neighbours(half):
        return at_first(half, peer(first[half], 1)), at_second(half, peer(second[half], 1))

    following, before = lax.rem(seg + 1, n_seg), lax.rem(seg + n_seg - 1, n_seg)

    barrier = pltpu.get_barrier_semaphore()
    for off in offsets(n):
        for half in range(2):
            pl.semaphore_signal(
                barrier,
                inc=1,
                device_id={"kv": at_first(half, peer(first[half], off))},
                device_id_type=MESH,
            )
    for other in (following, before):
        pl.semaphore_signal(barrier, inc=1, device_id={"segment": other}, device_id_type=MESH)

    loads = [
        pltpu.make_async_copy(src, dst, load_sem.at[i])
        for i, (src, dst) in enumerate(
            (
                (q_hbm, q_raw),
                (len_hbm, len_buf),
                (dev_hbm, dev_buf),
                (slot_hbm, slot_buf),
                (k_hbm, k_buf),
                (v_hbm, v_buf),
                (nk_hbm, nk_raw),
                (nv_hbm, nv_raw),
                (res_hbm, res_buf),
                (w_hbm.at[:, 0], w_buf.at[0]),
                (w_hbm.at[:, 1], w_buf.at[1]),
            )
        )
    ]
    for load in loads:
        load.start()

    loads[0].wait()
    heads_in_row(q_raw, rows64)
    for half in range(2):
        for p in range(2):
            start = half * HALF + p * PAIR
            q_ref[half, p] = rows64[start : start + PAIR, :].astype(bf16)
            q_all[half, second[half], p, first[half]] = q_ref[half, p]

    pl.semaphore_wait(barrier, 2 * (n - 1) + 2)

    def ask_first(half, i):
        mine = first[half]
        return copy(
            ASK_FIRST, half, q_ref.at[half], q_all.at[half, second[half], :, mine], at_first(half, i)
        )

    def asked(half):
        every = q_all.at[half, second[half], :, pl.ds(0, n - 1)]
        return copy(ASK_FIRST, half, every, every, neighbours(half)[0])

    def piece_of(ring, half, block, piece):
        if piece is None:
            return (q_all if ring == ASK_SECOND else told_all).at[half, block]
        if ring == ASK_SECOND:
            return q_all.at[half, block, piece]
        rows_of = HALF // 4
        return told_all.at[half, block, pl.ds(piece * rows_of, rows_of)]

    def leg_copy(ring, half, leg, block):
        ref = piece_of(ring, half, peer(second[half], n + block), LEGS[leg][1])
        return pltpu.make_async_remote_copy(
            src_ref=ref,
            dst_ref=ref,
            send_sem=leg_send.at[ring, half * len(LEGS) + leg],
            recv_sem=leg_recv.at[ring, half * len(LEGS) + leg],
            device_id={"kv": at_second(half, peer(second[half], n + LEGS[leg][2]))},
            device_id_type=MESH,
        )

    def leave(ring, half, leg):
        return leg_copy(ring, half, leg, LEGS[leg][0])

    def arrive(ring, half, leg):
        return leg_copy(ring, half, leg, LEGS[leg][3])

    def begin(ring, half):
        for leg in range(4):
            leave(ring, half, leg).start()

    def forward(ring, half):
        for way in range(2):
            arrive(ring, half, way).wait_recv()
            leave(ring, half, 4 + way).start()
        for way in range(2):
            leave(ring, half, 6 + way).start()

    for off in offsets(n):
        for half in range(2):
            ask_first(half, peer(first[half], off)).start()

    requests = n * n
    for load in loads[1:4]:
        load.wait()
    blocks = dev_buf.shape[1]
    holder = jnp.where(dev_buf[0] == me, slot_buf[0], -1)
    numbers = lax.broadcasted_iota(jnp.int32, (blocks, requests), 0)
    live = jnp.clip(len_buf[...] - numbers * BLK, 0, BLK).astype(f32)
    slot_of = lax.broadcasted_iota(jnp.int32, (slots, requests), 0)
    count = jnp.zeros((slots, requests), f32)
    for b in range(blocks):
        count = count + jnp.where(slot_of == holder[b : b + 1, :], live[b : b + 1, :], 0.0)
    spread = (
        lax.div(lax.broadcasted_iota(jnp.int32, (slots, tokens), 1), BLK)
        == lax.broadcasted_iota(jnp.int32, (slots, tokens), 0)
    ).astype(bf16)
    limit = lax.dot_general(
        count.astype(bf16), spread, (((0,), (0,)), ((), ())), preferred_element_type=f32
    )
    place = lax.rem(lax.broadcasted_iota(jnp.int32, (requests, tokens), 1), BLK).astype(f32)
    mask = jnp.where(place < limit, 0.0, EMPTY)
    for r in range(requests):
        bias_buf[r] = jnp.broadcast_to(mask[r : r + 1, :], (PAIR // 2, tokens))

    for half in range(2):
        asked(half).wait_recv()
        begin(ASK_SECOND, half)
    loads[4].wait()
    for pair in range(4):
        kt_buf[pair] = k_buf[:, :, pair * 256 : (pair + 1) * 256].reshape(tokens, 256).T
    loads[5].wait()

    def tiles(count):
        inside = lax.rem(lax.broadcasted_iota(jnp.int32, (count * PAIR, 128), 0), PAIR)
        return inside < PAIR // 2

    lane = lax.broadcasted_iota(jnp.int32, (PAIR // 2, 128), 1)
    used = 4 * n

    def three(stat):
        high = stat.astype(bf16).astype(f32)
        rest = stat - high
        middle = rest.astype(bf16).astype(f32)
        low = rest - middle
        return jnp.where(
            lane < used,
            high,
            jnp.where(lane < 2 * used, pltpu.roll(middle, used, 1), pltpu.roll(low, 2 * used, 1)),
        )

    def pack(above, below):
        return jnp.concatenate([three(above), three(below)], axis=0).astype(bf16)

    def unpack(tile):
        sides = tile.astype(f32)
        sides = (sides + pltpu.roll(sides, 128 - used, 1)) + pltpu.roll(sides, 128 - 2 * used, 1)
        return sides[: PAIR // 2], sides[PAIR // 2 :]

    def attend(half, those):
        count = len(those) * n
        upper = tiles(count)
        keep_upper = upper.astype(f32).astype(bf16)
        keep_lower = (1.0 - upper.astype(f32)).astype(bf16)
        bias = jnp.concatenate(
            [
                bias_buf[pl.ds(b * n, n)]
                if half == 0
                else jnp.stack([bias_buf[f * n + b] for f in range(n)], axis=0)
                for b in those
            ],
            axis=0,
        )
        tops = [jnp.full((PAIR // 2, 128), FLOOR, f32) for _ in those]
        totals = [jnp.zeros((PAIR // 2, 128), f32) for _ in those]
        for p in range(2):
            pair = half * 2 + p
            x = jnp.concatenate([q_all[half, b, p].reshape(rows, 128) for b in those], axis=0)
            x = jnp.concatenate([x * keep_upper, x * keep_lower], axis=1)
            score = jnp.dot(x, kt_buf[pair], preferred_element_type=f32)
            score = score.reshape(count, 2, PAIR // 2, tokens) + bias[:, None]
            score = score.reshape(count * PAIR, tokens)
            top = jnp.maximum(jnp.max(score, axis=1, keepdims=True), FLOOR)
            prob = jnp.exp2((score - top) * (SCALE * LOG2_E))
            total = jnp.sum(prob, axis=1, keepdims=True)
            value = v_buf[:, :, pair * 256 : (pair + 1) * 256].reshape(tokens, 256)
            acc = jnp.dot(prob.astype(bf16), value, preferred_element_type=f32)
            acc = jnp.where(upper, acc[:, :128], acc[:, 128:])
            acc = acc.astype(bf16).reshape(count, PAIR, 128)
            top = top.reshape(count, 2, PAIR // 2, 1)
            total = total.reshape(count, 2, PAIR // 2, 1)
            for k, b in enumerate(those):
                for r in range(n):
                    part[half, b, r * HALF + p * PAIR : r * HALF + (p + 1) * PAIR, :] = acc[k * n + r]
                    for side in range(2):
                        here = lane == (side * 2 + p) * n + r
                        tops[k] = jnp.where(here, top[k * n + r, side], tops[k])
                        totals[k] = jnp.where(here, total[k * n + r, side], totals[k])
        for k, b in enumerate(those):
            part[half, b, n * HALF :, :] = pack(tops[k], totals[k])

    def send_part(half, i):
        return copy(PART, half, part.at[half, i], got.at[half, second[half]], at_second(half, i))

    def parted(half):
        every = got.at[half, pl.ds(0, n - 1)]
        return copy(PART, half, every, every, neighbours(half)[1])

    for half in range(2):
        attend(half, [second[half]])
        got[half, second[half]] = part[half, second[half]]

    for half in range(2):
        forward(ASK_SECOND, half)

    def one_step(t, carry):
        @pl.when(t == 1)
        def _():
            for half in range(2):
                for leg in (2, 3):
                    arrive(ASK_SECOND, half, leg).wait_recv()

        @pl.when(t == 2)
        def _():
            for half in range(2):
                for leg in (4, 5):
                    arrive(ASK_SECOND, half, leg).wait_recv()

        away = lax.rem(t + 2, 3) + 1
        those = [
            [peer(second[half], n - away), peer(second[half], away)] for half in range(2)
        ]
        for half in range(2):
            attend(half, those[half])
        for half in range(2):
            for b in those[half]:
                send_part(half, b).start()
        return carry

    lax.fori_loop(0, 3, one_step, 0)
    for half in range(2):
        for leg in (6, 7):
            arrive(ASK_SECOND, half, leg).wait_recv()
        across = peer(second[half], n // 2)
        attend(half, [across])
        send_part(half, across).start()

    def send_merged(half, i):
        return copy(MERGED, half, merged.at[half, i], last.at[half, first[half]], at_first(half, i))

    def all_merged(half):
        every = last.at[half, pl.ds(0, n - 1)]
        return copy(MERGED, half, every, every, neighbours(half)[0])

    for half in range(2):
        parted(half).wait_recv()
        sides = [unpack(got[half, i, n * HALF :, :]) for i in range(n)]
        tops = jnp.stack([above for above, _ in sides], axis=0)
        totals = jnp.stack([below for _, below in sides], axis=0)
        top = jnp.max(tops, axis=0)
        weight = jnp.exp((tops - top[None]) * SCALE)
        total = jnp.sum(weight * totals, axis=0)
        some = jnp.maximum(total, 0.5)
        weight = weight / some[None]
        lse = jnp.where(total > 0.0, top * SCALE + jnp.log(some), EMPTY)
        tail = pack(lse, jnp.zeros_like(lse))
        for r in range(n):
            for p in range(2):
                scale = jnp.concatenate(
                    [
                        weight[:, :, (side * 2 + p) * n + r : (side * 2 + p) * n + r + 1]
                        for side in range(2)
                    ],
                    axis=1,
                )
                start = r * HALF + p * PAIR
                piece = got[half, :, start : start + PAIR, :].astype(f32)
                merged[half, r, p * PAIR : (p + 1) * PAIR, :] = jnp.sum(
                    piece * scale, axis=0
                ).astype(bf16)
            merged[half, r, HALF:, :] = tail
        for off in offsets(n):
            send_merged(half, peer(first[half], off)).start()
        last[half, first[half]] = merged[half, first[half]]

    def tell_first(half, i):
        return copy(TELL_FIRST, half, attn.at[half], told.at[half, first[half]], at_first(half, i))

    def all_told(half):
        every = told.at[half, pl.ds(0, n - 1)]
        return copy(TELL_FIRST, half, every, every, neighbours(half)[0])

    for load in loads[6:9]:
        load.wait()
    heads_in_row(nk_raw, rows64.at[pl.ds(0, KV_HEADS)])
    new_keys = rows64[:KV_HEADS, :]
    heads_in_row(nv_raw, rows64.at[pl.ds(KV_HEADS, KV_HEADS)])
    new_values = rows64[KV_HEADS : 2 * KV_HEADS, :]
    for half in range(2):
        kv_half = slice(half * 4, half * 4 + 4)
        query = q_ref[half].astype(f32).reshape(4, 8, 128)
        own = jnp.sum(query * new_keys[kv_half][:, None, :], axis=2, keepdims=True) * SCALE
        own = own.reshape(HALF, 1)
        own_value = jnp.broadcast_to(new_values[kv_half][:, None, :], (4, 8, 128)).reshape(HALF, 128)
        all_merged(half).wait_recv()
        lses = []
        for i in range(n):
            stat = unpack(last[half, i, HALF:, :])[0]
            lses.append(
                jnp.concatenate(
                    [
                        jnp.sum(
                            jnp.where(lane == (side * 2 + p) * n + first[half], stat, 0.0),
                            axis=1,
                            keepdims=True,
                        )
                        for p in range(2)
                        for side in range(2)
                    ],
                    axis=0,
                )
            )
        top = own
        for lse in lses:
            top = jnp.maximum(top, lse)
        weight = jnp.exp(own - top)
        total = weight
        acc = weight * own_value
        for i in range(n):
            weight = jnp.exp(lses[i] - top)
            total = total + weight
            acc = acc + weight * last[half, i, :HALF, :].astype(f32)
        attn[half] = (acc / total).astype(bf16)
        for off in offsets(n):
            tell_first(half, peer(first[half], off)).start()
        told[half, first[half]] = attn[half]

    for half in range(2):
        all_told(half).wait_recv()
        rows32[half] = told[half].astype(f32).reshape(n * HALF, 128)
        for h in range(HALF // 2):
            tile = [rows32[half, pl.ds(2 * h + s, n, stride=HALF), :] for s in range(2)]
            told_all[half, second[half], h] = jnp.concatenate(tile, axis=0).astype(bf16)
        begin(TELL_SECOND, half)

    for half in range(2):
        forward(TELL_SECOND, half)
    loads[9].wait()
    loads[10].wait()
    depth = HALF // 2 * HEAD_DIM
    mixed = []
    for half in range(2):
        for leg in range(2, len(LEGS)):
            arrive(TELL_SECOND, half, leg).wait_recv()
        x = jnp.concatenate(
            [told_all[half, :, h].reshape(n * 2 * n, 128) for h in range(HALF // 2)], axis=1
        )
        w = jnp.concatenate(
            [
                w_buf[side, half * (HALF // 2) : (half + 1) * (HALF // 2)].reshape(depth, 128)
                for side in range(2)
            ],
            axis=1,
        )
        acc = jnp.dot(x, w, preferred_element_type=f32).reshape(n, 2, n, 256)
        mixed.append(acc[:, 0, :, :128] + acc[:, 1, :, 128:])
    turn[...] = mixed[1].reshape(requests, 128)
    other = jnp.concatenate([turn[pl.ds(i, n, stride=n), :] for i in range(n)], axis=0)
    layer = res_buf[0].astype(f32) + (mixed[0].reshape(requests, 128) + other)
    line[...] = layer.astype(bf16)

    hand = pltpu.make_async_remote_copy(
        src_ref=line,
        dst_ref=landed,
        send_sem=pass_sem.at[0],
        recv_sem=pass_sem.at[1],
        device_id={"segment": following},
        device_id_type=MESH,
    )
    hand.start()

    for half in range(2):
        for stage in (asked, parted, all_merged, all_told):
            stage(half).wait_send()
        for ring in (ASK_SECOND, TELL_SECOND):
            for leg in range(len(LEGS)):
                leave(ring, half, leg).wait_send()
    hand.wait()
    out_ref[...] = landed[...]


def local(
    n_seg,
    n,
    queries,
    new_key,
    new_value,
    key_pool,
    value_pool,
    lengths,
    block_device,
    block_slot,
    residual,
    out_weight,
):
    f32, bf16 = jnp.float32, jnp.bfloat16
    slots = key_pool.shape[1]
    tokens = slots * BLK
    requests = n * n
    whole = pl.BlockSpec(memory_space=pltpu.VMEM)
    outside = pl.BlockSpec(memory_space=pltpu.HBM)
    blocks = block_device.shape[2]
    out = pl.pallas_call(
        functools.partial(kernel, n_seg, n),
        out_shape=jax.ShapeDtypeStruct((requests, 128), bf16),
        in_specs=[outside] * 10,
        out_specs=whole,
        scratch_shapes=[
            pltpu.VMEM((1, 1, HEADS * HEAD_DIM), bf16),
            pltpu.VMEM((1, 1, KV_HEADS * HEAD_DIM), bf16),
            pltpu.VMEM((1, 1, KV_HEADS * HEAD_DIM), bf16),
            pltpu.VMEM((1, requests), jnp.int32),
            pltpu.VMEM((1, blocks, requests), jnp.int32),
            pltpu.VMEM((1, blocks, requests), jnp.int32),
            pltpu.VMEM((1, requests, 128), bf16),
            pltpu.VMEM((HEADS, 128), f32),
            pltpu.VMEM((2, 2, PAIR, 128), bf16),
            pltpu.VMEM((slots, BLK, KV_HEADS * HEAD_DIM), bf16),
            pltpu.VMEM((slots, BLK, KV_HEADS * HEAD_DIM), bf16),
            pltpu.VMEM((2, HEADS // 2, HEAD_DIM, 128), bf16),
            pltpu.VMEM((4, 256, tokens), bf16),
            pltpu.VMEM((requests, PAIR // 2, tokens), f32),
            pltpu.VMEM((2, n, 2, n, PAIR, 128), bf16),
            pltpu.VMEM((2, n, n * HALF + PAIR, 128), bf16),
            pltpu.VMEM((2, n, n * HALF + PAIR, 128), bf16),
            pltpu.VMEM((2, n, HALF + PAIR, 128), bf16),
            pltpu.VMEM((2, n, HALF + PAIR, 128), bf16),
            pltpu.VMEM((2, HALF, 128), bf16),
            pltpu.VMEM((2, n, HALF, 128), bf16),
            pltpu.VMEM((2, n * HALF, 128), f32),
            pltpu.VMEM((2, n, HALF // 2, 2 * n, 128), bf16),
            pltpu.VMEM((requests, 128), f32),
            pltpu.VMEM((requests, 128), bf16),
            pltpu.VMEM((requests, 128), bf16),
            pltpu.SemaphoreType.DMA((4, 2)),
            pltpu.SemaphoreType.DMA((4, 2)),
            pltpu.SemaphoreType.DMA((2, 2 * len(LEGS))),
            pltpu.SemaphoreType.DMA((2, 2 * len(LEGS))),
            pltpu.SemaphoreType.DMA((11,)),
            pltpu.SemaphoreType.DMA((2,)),
        ],
        compiler_params=pltpu.CompilerParams(
            collective_id=0, has_side_effects=True, vmem_limit_bytes=60 * 1024 * 1024
        ),
        name="decode_layer",
    )(
        queries,
        new_key,
        new_value,
        lengths,
        jnp.swapaxes(block_device, 1, 2),
        jnp.swapaxes(block_slot, 1, 2),
        residual,
        key_pool[0],
        value_pool[0],
        out_weight[0].reshape(HEADS // 2, 2, HEAD_DIM, 128),
    )
    return out[None]


def solution(mesh):
    placed = (
        P("segment", "kv", None),
        P("segment", "kv", None),
        P("segment", "kv", None),
        P("segment", "kv", None, None),
        P("segment", "kv", None, None),
        P("segment", None),
        P("segment", None, None),
        P("segment", None, None),
        P("segment", None, "kv"),
        P("segment", None, "kv"),
    )
    n_seg = mesh.shape["segment"]
    n = next(i for i in range(1, 64) if i * i == mesh.shape["kv"])
    return jax.shard_map(
        functools.partial(local, n_seg, n),
        mesh=mesh,
        in_specs=placed,
        out_specs=P("segment", None, "kv"),
        check_vma=False,
    )
```

profile of v0, /device:TPU:1, one launch (start us, length us, event | category | flops | bytes accessed | tf_op | source)
XLA Modules:
  0.0 70.1 jit_solution(1534894074494038069)
XLA Ops:
  0.0 68.8 %decode_layer.1 = bf16[64,128]{1,0:T(8,128)(2,1)} custom-call(bf16[1,1,8192]{2,1,0:T(2,128)(2,1)} %q_hbm.1, bf16[1,1,1024]{2,1,0:T(2,128)(2,1)} %nk_hbm.1, bf16[1,1,1024]{2,1,0:T(2,128)(2,1)} %nv_hbm.1, s32[1,64]{1,0:T(1,128)} %len_hbm.1, s32[1,32,64]{2,1,0:T(8,128)} %bitcast.10, s32[1,32,64]{2,1,0:T(8,128)} %bitcast.11, bf16[1,64,128]{2,1,0:T(8,128)(2,1)} %res_hbm.1, ...), custom_call_target="tpu_custom_call" | custom-call | tf_op jit(solution)/shard_map/decode_layer/pallas_call | solution.py:535
  68.8 1.3 %copy.12 = bf16[1,64,128]{2,1,0:T(8,128)(2,1)} copy(bf16[1,64,128]{2,1,0:T(8,128)(2,1)} %bitcast.9) | data formatting | bytes 32768
where the time goes:
time: 70.3 us; the launch traced here: 70.1 us
  Pallas kernels  68.8 us (98%)
  local copies, waits for them, and re-layouts  1.32 us (2%)
    pallas_call x1, Pallas kernels, local(): pl.pallas_call(functools.partial(kernel, n_seg, n), out_shape=jax.ShapeDt...  68.8 us

commit v1 on v0

--- a/solution.py
+++ b/solution.py
@@ -329,10 +329,6 @@
         return copy(PART, half, every, every, neighbours(half)[1])
 
     for half in range(2):
-        attend(half, [second[half]])
-        got[half, second[half]] = part[half, second[half]]
-
-    for half in range(2):
         forward(ASK_SECOND, half)
 
     def one_step(t, carry):
@@ -354,7 +350,6 @@
         ]
         for half in range(2):
             attend(half, those[half])
-        for half in range(2):
             for b in those[half]:
                 send_part(half, b).start()
         return carry
@@ -366,6 +361,10 @@
         across = peer(second[half], n // 2)
         attend(half, [across])
         send_part(half, across).start()
+
+    for half in range(2):
+        attend(half, [second[half]])
+        got[half, second[half]] = part[half, second[half]]
 
     def send_merged(half, i):
         return copy(MERGED, half, merged.at[half, i], last.at[half, first[half]], at_first(half, i))

time: 70.3 us -> 69.5 us (0.989)
  Pallas kernels: 68.8 us -> 67.6 us
    pallas_call x1, Pallas kernels: 68.8 us -> 67.6 us  [local(): pl.pallas_call(functools.partial(kernel, n_seg, n), out_shape=jax.ShapeDt...]
where the time goes in v1:
time: 69.5 us; the launch traced here: 68.9 us
  Pallas kernels  67.6 us (97%)
  local copies, waits for them, and re-layouts  1.32 us (2%)
    pallas_call x1, Pallas kernels, local(): pl.pallas_call(functools.partial(kernel, n_seg, n), out_shape=jax.ShapeDt...  67.6 us

profile of v1, /device:TPU:1, one launch (start us, length us, event | category | flops | bytes accessed | tf_op | source)
XLA Modules:
  0.0 68.9 jit_solution(2586340626383143521)
XLA Ops:
  0.0 67.6 %decode_layer.1 = bf16[64,128]{1,0:T(8,128)(2,1)} custom-call(bf16[1,1,8192]{2,1,0:T(2,128)(2,1)} %q_hbm.1, bf16[1,1,1024]{2,1,0:T(2,128)(2,1)} %nk_hbm.1, bf16[1,1,1024]{2,1,0:T(2,128)(2,1)} %nv_hbm.1, s32[1,64]{1,0:T(1,128)} %len_hbm.1, s32[1,32,64]{2,1,0:T(8,128)} %bitcast.10, s32[1,32,64]{2,1,0:T(8,128)} %bitcast.11, bf16[1,64,128]{2,1,0:T(8,128)(2,1)} %res_hbm.1, ...), custom_call_target="tpu_custom_call" | custom-call | tf_op jit(solution)/shard_map/decode_layer/pallas_call | solution.py:534
  67.6 1.3 %copy.12 = bf16[1,64,128]{2,1,0:T(8,128)(2,1)} copy(bf16[1,64,128]{2,1,0:T(8,128)(2,1)} %bitcast.9) | data formatting | bytes 32768

commit v2 on v1

--- a/solution.py
+++ b/solution.py
@@ -349,8 +349,8 @@
             [peer(second[half], n - away), peer(second[half], away)] for half in range(2)
         ]
         for half in range(2):
-            attend(half, those[half])
             for b in those[half]:
+                attend(half, [b])
                 send_part(half, b).start()
         return carry
 

time: 69.5 us -> 69.9 us (level)
  Pallas kernels: 67.6 us -> 68.3 us
    pallas_call x1, Pallas kernels: 67.6 us -> 68.3 us  [local(): pl.pallas_call(functools.partial(kernel, n_seg, n), out_shape=jax.ShapeDt...]
where the time goes in v2:
time: 69.9 us; the launch traced here: 69.7 us
  Pallas kernels  68.3 us (98%)
  local copies, waits for them, and re-layouts  1.32 us (2%)
    pallas_call x1, Pallas kernels, local(): pl.pallas_call(functools.partial(kernel, n_seg, n), out_shape=jax.ShapeDt...  68.3 us

profile of v2, /device:TPU:1, one launch (start us, length us, event | category | flops | bytes accessed | tf_op | source)
XLA Modules:
  0.0 69.7 jit_solution(14614817650315477324)
XLA Ops:
  0.0 68.3 %decode_layer.1 = bf16[64,128]{1,0:T(8,128)(2,1)} custom-call(bf16[1,1,8192]{2,1,0:T(2,128)(2,1)} %q_hbm.1, bf16[1,1,1024]{2,1,0:T(2,128)(2,1)} %nk_hbm.1, bf16[1,1,1024]{2,1,0:T(2,128)(2,1)} %nv_hbm.1, s32[1,64]{1,0:T(1,128)} %len_hbm.1, s32[1,32,64]{2,1,0:T(8,128)} %bitcast.10, s32[1,32,64]{2,1,0:T(8,128)} %bitcast.11, bf16[1,64,128]{2,1,0:T(8,128)(2,1)} %res_hbm.1, ...), custom_call_target="tpu_custom_call" | custom-call | tf_op jit(solution)/shard_map/decode_layer/pallas_call | solution.py:534
  68.3 1.3 %copy.12 = bf16[1,64,128]{2,1,0:T(8,128)(2,1)} copy(bf16[1,64,128]{2,1,0:T(8,128)(2,1)} %bitcast.9) | data formatting | bytes 32768

commit v3 on v2

--- a/solution.py
+++ b/solution.py
@@ -354,13 +354,14 @@
                 send_part(half, b).start()
         return carry
 
-    lax.fori_loop(0, 3, one_step, 0)
+    lax.fori_loop(0, 2, one_step, 0)
     for half in range(2):
         for leg in (6, 7):
             arrive(ASK_SECOND, half, leg).wait_recv()
         across = peer(second[half], n // 2)
         attend(half, [across])
         send_part(half, across).start()
+    lax.fori_loop(2, 3, one_step, 0)
 
     for half in range(2):
         attend(half, [second[half]])

time: 69.9 us -> 69.5 us (level)
  Pallas kernels: 68.3 us -> 67.5 us
    pallas_call x1, Pallas kernels: 68.3 us -> 67.5 us  [local(): pl.pallas_call(functools.partial(kernel, n_seg, n), out_shape=jax.ShapeDt...]
where the time goes in v3:
time: 69.5 us; the launch traced here: 68.9 us
  Pallas kernels  67.5 us (97%)
  local copies, waits for them, and re-layouts  1.32 us (2%)
    pallas_call x1, Pallas kernels, local(): pl.pallas_call(functools.partial(kernel, n_seg, n), out_shape=jax.ShapeDt...  67.5 us

profile of v3, /device:TPU:1, one launch (start us, length us, event | category | flops | bytes accessed | tf_op | source)
XLA Modules:
  0.0 68.9 jit_solution(557690464981960487)
XLA Ops:
  0.0 67.5 %decode_layer.1 = bf16[64,128]{1,0:T(8,128)(2,1)} custom-call(bf16[1,1,8192]{2,1,0:T(2,128)(2,1)} %q_hbm.1, bf16[1,1,1024]{2,1,0:T(2,128)(2,1)} %nk_hbm.1, bf16[1,1,1024]{2,1,0:T(2,128)(2,1)} %nv_hbm.1, s32[1,64]{1,0:T(1,128)} %len_hbm.1, s32[1,32,64]{2,1,0:T(8,128)} %bitcast.10, s32[1,32,64]{2,1,0:T(8,128)} %bitcast.11, bf16[1,64,128]{2,1,0:T(8,128)(2,1)} %res_hbm.1, ...), custom_call_target="tpu_custom_call" | custom-call | tf_op jit(solution)/shard_map/decode_layer/pallas_call | solution.py:535
  67.6 1.3 %copy.12 = bf16[1,64,128]{2,1,0:T(8,128)(2,1)} copy(bf16[1,64,128]{2,1,0:T(8,128)(2,1)} %bitcast.9) | data formatting | bytes 32768
